TPU v7x, 32 devices: a whole 2x2x4 slice. The times are simulated.
32 devices in a mesh: groups: 2 (over y), ep: 4 (over x, core), tp: 4 (over z).
Axes of the slice: x: 2, y: 2, z: 4, core: 2. Of those that a mesh axis runs over, the one named last changes fastest.
Arguments:
- tokens: bfloat16 [1024, 6144], P(('groups', 'ep'), 'tp'), parts along dimension 0, may hold values from -6 to 6
- picks: int32 [1024, 2], P(('groups', 'ep')), parts along dimension 0, may hold values from 0 to 3, all different within a row; in each aligned block of 128 rows (0 to 127, 128 to 255, ...) at most 80 rows name the same one
- gates: float32 [1024, 2], P(('groups', 'ep')), parts along dimension 0, may hold values from 0.1 to 1
- counts: int32 [8], P(('groups', 'ep')), parts along dimension 0, may hold values from 64 to 128, as said below
- gate_weight: bfloat16 [6144, 32768], P(None, ('ep', 'tp')), may hold values from -0.078125 to 0.078125
- up_weight: bfloat16 [6144, 32768], P(None, ('ep', 'tp')), may hold values from -0.078125 to 0.078125
- down_weight: bfloat16 [32768, 6144], P('ep', 'tp'), may hold values from -0.0625 to 0.0625
Outputs:
- mixed: bfloat16 [1024, 6144], P(('groups', 'ep'), 'tp'), parts along dimension 0
There are 2 independent parts, one for each index of `groups`. A program takes and returns all parts, laid end to end along the dimension named above; an argument that names none is the same for every part. Nothing has to cross between parts.
Inputs may be any that keep to these rules, and one draw needn't show every extreme that they name: The two picks of a row differ; among the rows of one index of ep no expert is named by more than 80 rows. `counts`: some index of ep has all 128 rows valid; valid rows come first in each block.
All inputs are finite; a program needn't handle non-finite values.
Results may differ from a plain program's by a relative error of at most 0.005.
Values may be sent and summed in bfloat16 or wider, within the bound.
A program may use at most 192 MiB of HBM per device.

v0:
```python
import jax
import jax.numpy as jnp
from jax import lax
from jax.sharding import PartitionSpec as P

E = 4
CAP = 80


def body(tokens, picks, gates, counts, gate_weight, up_weight, down_weight):
    ep_count = lax.axis_size("ep")
    copies = ep_count // E
    row_count = tokens.shape[0]
    capacity = CAP
    live_rows = jnp.arange(row_count) < counts[0]
    matches = picks[:, :, None] == jnp.arange(E, dtype=jnp.int32)[None, None, :]
    routed = jnp.any(matches, axis=1) & live_rows[:, None]
    row_weight = jnp.sum(jnp.where(matches, gates[:, :, None], 0.0), axis=1)
    slot_rank = jnp.cumsum(routed.astype(jnp.int32), axis=0) - 1
    placed = routed[None] & (
        slot_rank[None] == jnp.arange(capacity, dtype=jnp.int32)[:, None, None]
    )
    placed = jnp.transpose(placed, (2, 0, 1))
    onehot = placed.astype(jnp.bfloat16)
    gathered = lax.all_gather(tokens, "tp", axis=1, tiled=True)
    packed = jnp.einsum("ecr,rf->ecf", onehot, gathered, preferred_element_type=jnp.float32).astype(
        jnp.bfloat16
    )
    arrived = lax.all_to_all(
        jnp.repeat(packed, copies, axis=0), "ep", split_axis=0, concat_axis=0, tiled=True
    )
    flat_rows = arrived.reshape(-1, arrived.shape[2])
    pre_gate = jnp.dot(flat_rows, gate_weight, preferred_element_type=jnp.float32)
    pre_up = jnp.dot(flat_rows, up_weight, preferred_element_type=jnp.float32)
    hidden = (jax.nn.silu(pre_gate) * pre_up).astype(jnp.bfloat16)
    partial_value = jnp.dot(
        lax.all_gather(hidden, "tp", axis=1, tiled=True),
        down_weight,
        preferred_element_type=jnp.float32,
    )
    returned = lax.all_to_all(
        partial_value.reshape(ep_count, capacity, partial_value.shape[1]),
        "ep",
        split_axis=0,
        concat_axis=0,
        tiled=True,
    )
    summed = jnp.sum(returned.reshape(E, copies, capacity, returned.shape[2]), axis=1)
    combine = placed.astype(jnp.float32) * jnp.transpose(row_weight)[:, None, :]
    mixed = jnp.einsum("ecr,ecf->rf", combine, summed, precision=lax.Precision.HIGHEST)
    return mixed.astype(jnp.bfloat16)


def solution(mesh):
    in_specs = (
        P(("groups", "ep"), "tp"),
        P(("groups", "ep"), None),
        P(("groups", "ep"), None),
        P(("groups", "ep")),
        P(None, ("ep", "tp")),
        P(None, ("ep", "tp")),
        P("ep", "tp"),
    )
    out_specs = P(("groups", "ep"), "tp")
    return jax.shard_map(body, mesh=mesh, in_specs=in_specs, out_specs=out_specs, check_vma=False)
```

profile of v0, /device:TPU:0, one launch (start us, length us, event | category | flops | bytes accessed | tf_op | source)
XLA Modules:
  0.0 275.8 jit_solution(331855305285048185)
XLA Ops:
  6.5 0.0 all-gather.3.cloned.1.call-start
  6.5 0.7 all-gather.3.cloned.1.call-update
  7.3 0.0 all-gather.5.cloned.1.call-start
  8.0 0.7 fusion.13
  8.7 0.1 copy.12
  8.8 0.2 reduce_window_sum.11
  9.0 0.1 copy.13
  9.0 39.7 %all-gather.3.cloned.1.call-done = bf16[128,6144]{1,0:T(8,128)(2,1)} async-done(((bf16[128,1536]{1,0:T(8,128)(2,1)}), bf16[128,6144]{1,0:T(8,128)(2,1)}) %all-gather.3.cloned.1.call-update) | async-done | bytes 1572880 | tf_op jit(solution)/shard_map/all_gather | solution.py:25
  48.8 2.6 convolution_convert_fusion
  51.3 47.9 %all_to_all.10 = bf16[4,80,6144]{2,1,0:T(8,128)(2,1)S(1)} all-to-all(bf16[4,80,6144]{2,1,0:T(8,128)(2,1)S(1)} %convolution_convert_fusion), channel_id=1, replica_groups=mesh['groups'=2,'ep'=4,'tp'=4] {'ep'}, dimensions={0} | all-to-all | bytes 7864320 | tf_op jit(solution)/shard_map/all_to_all | solution.py:29
  99.2 13.2 %fusion.15 = f32[320,2048]{1,0:T(8,128)S(1)} fusion(bf16[320,6144]{1,0:T(8,128)(2,1)S(1)} %bitcast.23, bf16[6144,2048]{1,0:T(8,128)(2,1)} %param.11), kind=kOutput, calls=%fused_computation.23 | convolution fusion | flops 8053063680 | bytes 31719424 | tf_op jit(solution)/shard_map/dot_general | solution.py:33
  112.4 14.4 %fusion = bf16[320,2048]{1,0:T(8,128)(2,1)} fusion(bf16[320,6144]{1,0:T(8,128)(2,1)S(1)} %bitcast.24, bf16[6144,2048]{1,0:T(8,128)(2,1)} %param.12, f32[320,2048]{1,0:T(8,128)S(1)} %fusion.15), kind=kOutput, calls=%fused_computation.2 | convolution fusion | flops 8056995840 | bytes 33030144 | tf_op jit(solution)/shard_map/dot_general | solution.py:34
  126.9 0.0 all-gather.5.cloned.1.call-update
  126.9 96.2 %all-gather.5.cloned.1.call-done = bf16[320,8192]{1,0:T(8,128)(2,1)} async-done(((bf16[320,2048]{1,0:T(8,128)(2,1)}), bf16[320,8192]{1,0:T(8,128)(2,1)}) %all-gather.5.cloned.1.call-update) | async-done | bytes 5242896 | tf_op jit(solution)/shard_map/all_gather | solution.py:37
  223.1 15.6 %fusion.16 = f32[320,1536]{1,0:T(8,128)} fusion(bf16[320,8192]{1,0:T(8,128)(2,1)} %all-gather.5.cloned.1.call-done, bf16[8192,1536]{1,0:T(8,128)(2,1)} %param.13), kind=kOutput, calls=%fused_computation.24 | convolution fusion | flops 8053063680 | bytes 32374784 | tf_op jit(solution)/shard_map/dot_general | solution.py:36
  238.7 0.0 copy-start
  238.7 0.0 copy-start.1
  238.7 3.7 %all-to-all-start.1 = ((f32[4,80,1536]{2,1,0:T(8,128)}), f32[4,80,1536]{2,1,0:T(8,128)S(1)}, u32[]{:S(2)}, u32[]{:S(2)}) async-start(f32[4,80,1536]{2,1,0:T(8,128)} %bitcast.25), calls=%async_computation.1 | async-start | bytes 3932160 | tf_op jit(solution)/shard_map/all_to_all | solution.py:41
  242.4 0.0 copy-done
  242.4 0.0 copy-done.1
  242.4 24.2 %all-to-all-done.1 = f32[4,80,1536]{2,1,0:T(8,128)S(1)} async-done(((f32[4,80,1536]{2,1,0:T(8,128)}), f32[4,80,1536]{2,1,0:T(8,128)S(1)}, u32[]{:S(2)}, u32[]{:S(2)}) %all-to-all-start.1) | async-done | bytes 1966112 | tf_op jit(solution)/shard_map/all_to_all | solution.py:41
  266.7 2.3 fusion.1
  (4 shorter events, 0.0 us)
Async XLA Ops:
  6.5 42.2 %all-gather.3.cloned.1.call-start = ((), (), s32[]{:S(2)}) async-start(), calls=%async_computation.2 | async-start | bytes 1966080 | tf_op jit(solution)/shard_map/all_gather | solution.py:25
  7.3 215.8 %all-gather.5.cloned.1.call-start = ((), (), s32[]{:S(2)}) async-start(), calls=%async_computation.3 | async-start | bytes 6553600 | tf_op jit(solution)/shard_map/all_gather | solution.py:37
  238.7 3.7 %copy-start = (s32[128,2]{0,1:T(2,128)S(1)}, s32[128,2]{0,1:T(2,128)}, u32[]{:S(2)}) copy-start(s32[128,2]{0,1:T(2,128)} %param.8) | copy-start | bytes 3076
  238.7 3.7 %copy-start.1 = (f32[128,2]{0,1:T(2,128)S(1)}, f32[128,2]{0,1:T(2,128)}, u32[]{:S(2)}) copy-start(f32[128,2]{0,1:T(2,128)} %param.9) | copy-start | bytes 3076
  238.7 28.0 %all-to-all-start.1 = ((f32[4,80,1536]{2,1,0:T(8,128)}), f32[4,80,1536]{2,1,0:T(8,128)S(1)}, u32[]{:S(2)}, u32[]{:S(2)}) async-start(f32[4,80,1536]{2,1,0:T(8,128)} %bitcast.25), calls=%async_computation.1 | async-start | bytes 3932160 | tf_op jit(solution)/shard_map/all_to_all | solution.py:41
Sparse Core Ops, SparseCore 0:
  8.9 39.7 all-gather.2
  127.0 96.0 all-gather.4
where the time goes:
time: 276 us
  waiting for transfers between devices  161 us (58%)
  matrix products  48.1 us (17%)
  blocking collectives  47.9 us (17%)
  between operations  14.1 us (5%)
  starting transfers between devices  3.77 us (1%)
    all_gather x1, waiting for transfers between devices, body(): lax.all_gather(hidden, 'tp', axis=1, tiled=True)  96.2 us
    all_to_all x1, blocking collectives, body(): lax.all_to_all(jnp.repeat(packed, copies, axis=0), 'ep', split_axis=0, co...  47.9 us
    all_gather x1, waiting for transfers between devices, body(): gathered = lax.all_gather(tokens, 'tp', axis=1, tiled=True)  39.7 us
    all_to_all x1, waiting for transfers between devices, body(): lax.all_to_all(partial_value.reshape(ep_count, capacity, partial_value.sh...  24.2 us
    dot_general x1, matrix products, body(): jnp.dot(lax.all_gather(hidden, 'tp', axis=1, tiled=True), down_weight, pr...  15.6 us
    dot_general x1, matrix products, body(): pre_up = jnp.dot(flat_rows, up_weight, preferred_element_type=jnp.float32)  14.4 us
    dot_general x1, matrix products, body(): jnp.dot(flat_rows, gate_weight, preferred_element_type=jnp.float32)  13.2 us
  transfers between devices with their start and end apart: 3, of which 3 were waited for; matrix products, arithmetic and copies ran while one was open for 0% of the time, Pallas kernels for 0%

commit v1 on v0

v1 whole, which is shorter than its diff:
```python
import functools

import jax
import jax.numpy as jnp
from jax import lax
from jax.experimental import pallas as pl
from jax.experimental.pallas import tpu as pltpu
from jax.sharding import PartitionSpec as P

E = 4
CAP = 80
MESH = pl.DeviceIdType.MESH


def gather_kernel(n_ep, n_tp, halves, tok, meta, out, meta_out, local_sem, z_send, x_send, c_send, recv, m_send, m_recv):
    z = lax.axis_index("tp")
    b = lax.axis_index("ep")
    chips = n_ep // 2
    rows, width = tok.shape
    part_rows = rows // halves
    partner = b + 1 - 2 * lax.rem(b, 2)
    peers = [2 * lax.rem(b // 2 + j, chips) + lax.rem(b, 2) for j in range(1, chips)]
    others = [lax.rem(b + j, n_ep) for j in range(1, n_ep)]

    def piece(block, p, h):
        return out.at[block, pl.ds(h * part_rows, part_rows), pl.ds(pl.multiple_of(p * width, 128), width)]

    def copy(block, p, h, own, send, device):
        src = tok.at[pl.ds(h * part_rows, part_rows), :] if own else piece(block, p, h)
        return pltpu.make_async_remote_copy(
            src_ref=src, dst_ref=piece(block, p, h), send_sem=send, recv_sem=recv.at[block, p, h],
            device_id=device, device_id_type=MESH)

    def right(p, h, own=False):
        return copy(b, p, h, own, z_send.at[0, p, h], {"tp": z + 1})

    def left(p, h, own=False):
        return copy(b, p, h, own, z_send.at[1, p, h], {"tp": z - 1})

    def across(j, p, h, own=False):
        return copy(b, p, h, own, x_send.at[j, p, h], {"ep": peers[j]})

    def to_core(block, p, h, own=False):
        return copy(block, p, h, own, c_send.at[block, p, h], {"ep": partner})

    def meta_copy(j):
        return pltpu.make_async_remote_copy(
            src_ref=meta, dst_ref=meta_out.at[b], send_sem=m_send.at[j], recv_sem=m_recv.at[b],
            device_id={"ep": others[j]}, device_id_type=MESH)

    local = pltpu.make_async_copy(tok, out.at[b, :, pl.ds(pl.multiple_of(z * width, 128), width)], local_sem.at[0])
    local_meta = pltpu.make_async_copy(meta, meta_out.at[b], local_sem.at[1])

    barrier = pltpu.get_barrier_semaphore()
    for other in others:
        pl.semaphore_signal(barrier, inc=1, device_id={"ep": other}, device_id_type=MESH)

    @pl.when(z > 0)
    def _():
        pl.semaphore_signal(barrier, inc=1, device_id={"tp": z - 1}, device_id_type=MESH)

    @pl.when(z < n_tp - 1)
    def _():
        pl.semaphore_signal(barrier, inc=1, device_id={"tp": z + 1}, device_id_type=MESH)

    pl.semaphore_wait(barrier, n_ep - 1 + jnp.minimum(z, 1) + jnp.minimum(n_tp - 1 - z, 1))

    def fan_out(p, h, own):
        for j in range(chips - 1):
            across(j, p, h, own).start()
        to_core(b, p, h, own).start()

    for h in range(halves):
        @pl.when(z < n_tp - 1)
        def _():
            right(z, h, True).start()

        @pl.when(z > 0)
        def _():
            left(z, h, True).start()

        fan_out(z, h, True)
    for j in range(n_ep - 1):
        meta_copy(j).start()
    local.start()
    local_meta.start()

    def pass_to_core(k, h):
        for p, there in ((z - k, z - k >= 0), (z + k, z + k < n_tp))[: 1 if k == 0 else 2]:
            @pl.when(there)
            def _():
                for block in peers:
                    to_core(block, p, h).wait_recv()
                    to_core(block, p, h).start()

    for k in range(1, n_tp):
        for h in range(halves):
            @pl.when(z - k >= 0)
            def _():
                right(z - k, h).wait_recv()

                @pl.when(z < n_tp - 1)
                def _():
                    right(z - k, h).start()

                fan_out(z - k, h, False)

            @pl.when(z + k < n_tp)
            def _():
                left(z + k, h).wait_recv()

                @pl.when(z > 0)
                def _():
                    left(z + k, h).start()

                fan_out(z + k, h, False)

            pass_to_core(k - 1, h)
    for h in range(halves):
        pass_to_core(n_tp - 1, h)

    for p in range(n_tp):
        for h in range(halves):
            for block in [partner] + [peer + partner - b for peer in peers]:
                to_core(block, p, h).wait_recv()
            for block in [b] + peers:
                to_core(block, p, h).wait_send()
            for j in range(chips - 1):
                across(j, p, h).wait_send()

            @pl.when((z < n_tp - 1) & (p <= z))
            def _():
                right(p, h).wait_send()

            @pl.when((z > 0) & (p >= z))
            def _():
                left(p, h).wait_send()
    for j in range(n_ep - 1):
        meta_copy(j).wait_send()
        pltpu.make_async_remote_copy(
            src_ref=meta, dst_ref=meta_out.at[others[j]], send_sem=m_send.at[j], recv_sem=m_recv.at[others[j]],
            device_id={"ep": others[j]}, device_id_type=MESH).wait_recv()
    local.wait()
    local_meta.wait()


def gather_tokens(tokens, meta, n_ep, n_tp):
    rows, width = tokens.shape
    halves = 2 if n_ep * n_tp <= 16 else 1
    dma = pltpu.SemaphoreType.DMA
    hbm = pl.BlockSpec(memory_space=pl.ANY)
    return pl.pallas_call(
        functools.partial(gather_kernel, n_ep, n_tp, halves),
        out_shape=(jax.ShapeDtypeStruct((n_ep, rows, n_tp * width), tokens.dtype),
                   jax.ShapeDtypeStruct((n_ep,) + meta.shape, meta.dtype)),
        in_specs=[hbm, hbm],
        out_specs=(hbm, hbm),
        scratch_shapes=[dma((2,)), dma((2, n_tp, halves)), dma((max(1, n_ep // 2 - 1), n_tp, halves)),
                        dma((n_ep, n_tp, halves)), dma((n_ep, n_tp, halves)), dma((n_ep,)), dma((n_ep,))],
        compiler_params=pltpu.CompilerParams(collective_id=0, has_side_effects=True),
        name="gather_tokens",
    )(tokens, meta)


def ffn_kernel(n_tp, cols, x, gate, up, down, out, wg, wu, wd, hid, acc, w_sem, d_sem, r_send, l_send, recv):
    z = lax.axis_index("tp")
    steps = hid.shape[1]
    depth = steps * cols

    def fetch(c, slot):
        at = pl.ds(pl.multiple_of(c * cols, 128), cols)
        return (pltpu.make_async_copy(gate.at[:, at], wg.at[slot], w_sem.at[0, slot]),
                pltpu.make_async_copy(up.at[:, at], wu.at[slot], w_sem.at[1, slot]))

    def fetch_down(s):
        at = pl.ds(pl.multiple_of(s * depth, 128), depth)
        return pltpu.make_async_copy(down.at[at, :], wd.at[at, :], d_sem.at[s])

    def send(s, c, sem, to):
        return pltpu.make_async_remote_copy(
            src_ref=hid.at[s, c], dst_ref=hid.at[s, c], send_sem=sem.at[s, c], recv_sem=recv.at[s, c],
            device_id={"tp": to}, device_id_type=MESH)

    def right(s, c):
        return send(s, c, r_send, z + 1)

    def left(s, c):
        return send(s, c, l_send, z - 1)

    for copy in fetch(0, 0):
        copy.start()
    acc[...] = jnp.zeros_like(acc)

    barrier = pltpu.get_barrier_semaphore()

    @pl.when(z > 0)
    def _():
        pl.semaphore_signal(barrier, inc=1, device_id={"tp": z - 1}, device_id_type=MESH)

    @pl.when(z < n_tp - 1)
    def _():
        pl.semaphore_signal(barrier, inc=1, device_id={"tp": z + 1}, device_id_type=MESH)

    pl.semaphore_wait(barrier, jnp.minimum(z, 1) + jnp.minimum(n_tp - 1 - z, 1))

    @pl.loop(0, steps)
    def _(c):
        slot = lax.rem(c, 2)

        @pl.when(c + 1 < steps)
        def _():
            for copy in fetch(c + 1, 1 - slot):
                copy.start()

        for copy in fetch(c, slot):
            copy.wait()
        pre_gate = jnp.dot(x[...], wg[slot], preferred_element_type=jnp.float32)
        pre_up = jnp.dot(x[...], wu[slot], preferred_element_type=jnp.float32)
        hid[z, c] = (pre_gate / (1.0 + jnp.exp(-pre_gate)) * pre_up).astype(hid.dtype)

        @pl.when(z < n_tp - 1)
        def _():
            right(z, c).start()

        @pl.when(z > 0)
        def _():
            left(z, c).start()

        @pl.when(c == max(0, steps - 2))
        def _():
            for s in range(n_tp):
                fetch_down(s).start()

    for s in range(n_tp):
        fetch_down(s).wait()

    def add(s, c):
        at = pl.ds(pl.multiple_of(s * depth + c * cols, 128), cols)
        acc[...] += jnp.dot(hid[s, c], wd[at, :], preferred_element_type=jnp.float32)

    for k in range(1, n_tp):
        @pl.loop(0, steps)
        def _(c):
            @pl.when(z - k >= 0)
            def _():
                right(z - k, c).wait_recv()

                @pl.when(z < n_tp - 1)
                def _():
                    right(z - k, c).start()

            @pl.when(z + k < n_tp)
            def _():
                left(z + k, c).wait_recv()

                @pl.when(z > 0)
                def _():
                    left(z + k, c).start()

            if k == 1:
                add(z, c)

            @pl.when(z - k >= 0)
            def _():
                add(z - k, c)

            @pl.when(z + k < n_tp)
            def _():
                add(z + k, c)

    out[...] = acc[...].astype(out.dtype)

    @pl.loop(0, steps)
    def _(c):
        for s in range(n_tp):
            @pl.when((z < n_tp - 1) & (s <= z))
            def _():
                right(s, c).wait_send()

            @pl.when((z > 0) & (s >= z))
            def _():
                left(s, c).wait_send()


def ffn(x, gate, up, down, n_tp):
    rows, width = x.shape
    hidden = gate.shape[1]
    cols = min(256, hidden)
    steps = hidden // cols
    dma = pltpu.SemaphoreType.DMA
    hbm = pl.BlockSpec(memory_space=pl.ANY)
    vmem = pl.BlockSpec(memory_space=pltpu.VMEM)
    bf16 = jnp.bfloat16
    return pl.pallas_call(
        functools.partial(ffn_kernel, n_tp, cols),
        out_shape=jax.ShapeDtypeStruct((rows, down.shape[1]), bf16),
        in_specs=[vmem, hbm, hbm, hbm],
        out_specs=vmem,
        scratch_shapes=[
            pltpu.VMEM((2, width, cols), bf16), pltpu.VMEM((2, width, cols), bf16),
            pltpu.VMEM(down.shape, bf16),
            pltpu.VMEM((n_tp, steps, rows, cols), bf16),
            pltpu.VMEM((rows, down.shape[1]), jnp.float32),
            dma((2, 2)), dma((n_tp,)), dma((n_tp, steps)), dma((n_tp, steps)), dma((n_tp, steps))],
        compiler_params=pltpu.CompilerParams(
            collective_id=1, has_side_effects=True, vmem_limit_bytes=60 * 1024 * 1024),
        cost_estimate=pl.CostEstimate(
            flops=2 * rows * (2 * width * hidden + down.size),
            bytes_accessed=2 * (gate.size + up.size + down.size), transcendentals=rows * hidden),
        name="ffn",
    )(x, gate, up, down)


def body(tokens, picks, gates, counts, gate_weight, up_weight, down_weight):
    n_ep, n_tp = lax.axis_size("ep"), lax.axis_size("tp")
    copies = n_ep // E
    row_count = tokens.shape[0]
    live = jnp.arange(row_count) < counts[0]
    meta = jnp.full((8, row_count), -1, jnp.int32).at[:2].set(jnp.where(live[None], picks.T, -1))
    gathered, meta_all = gather_tokens(tokens, meta, n_ep, n_tp)
    slots = jnp.arange(CAP, dtype=jnp.int32)

    expert = lax.axis_index("ep") // copies
    routed = jnp.any(meta_all[:, :2] == expert, axis=1)
    rank = jnp.cumsum(routed.astype(jnp.int32), axis=1) - 1
    onehot = (routed[:, None] & (rank[:, None] == slots[None, :, None])).astype(jnp.bfloat16)
    packed = jnp.einsum("bcr,brf->bcf", onehot, gathered, preferred_element_type=jnp.float32)
    packed = packed.astype(jnp.bfloat16).reshape(n_ep * CAP, -1)

    partial_value = ffn(packed, gate_weight, up_weight, down_weight, n_tp)
    returned = lax.all_to_all(
        partial_value.reshape(n_ep, CAP, -1), "ep", split_axis=0, concat_axis=0, tiled=True)

    matches = picks[:, :, None] == jnp.arange(E, dtype=jnp.int32)
    own_routed = jnp.any(matches, axis=1) & live[:, None]
    row_weight = jnp.sum(jnp.where(matches, gates[:, :, None], 0.0), axis=1)
    own_rank = jnp.cumsum(own_routed.astype(jnp.int32), axis=0) - 1
    placed = (own_routed.T[:, None] & (own_rank.T[:, None] == slots[None, :, None]))
    combine = placed.astype(jnp.float32) * row_weight.T[:, None, :]
    summed = jnp.sum(returned.reshape(E, copies, CAP, -1).astype(jnp.float32), axis=1)
    mixed = jnp.einsum("ecr,ecf->rf", combine, summed, precision=lax.Precision.HIGHEST)
    return mixed.astype(jnp.bfloat16)


def solution(mesh):
    rows = P(("groups", "ep"), None)
    in_specs = (
        P(("groups", "ep"), "tp"), rows, rows, P(("groups", "ep")),
        P(None, ("ep", "tp")), P(None, ("ep", "tp")), P("ep", "tp"),
    )
    out_specs = P(("groups", "ep"), "tp")
    return jax.shard_map(body, mesh=mesh, in_specs=in_specs, out_specs=out_specs, check_vma=False)
```

time: 276 us -> 166 us (0.60)
  waiting for transfers between devices: 161 us -> 13.3 us
  Pallas kernels: 0 us -> 138 us
  blocking collectives: 47.9 us -> 0 us
  matrix products: 48.1 us -> 7.48 us
  between operations: 14.1 us -> 0.72 us
    pallas_call x0 -> x2, Pallas kernels: none -> 138 us  [the longest x1 96.8 us: ffn(): pl.pallas_call(functools.partial(ffn_kernel, n_tp, cols), out_shape=jax.S...]
    all_gather x2 -> x0, waiting for transfers between devices: 136 us -> none  [the longest x1 96.2 us: body(): lax.all_gather(hidden, 'tp', axis=1, tiled=True)]
    all_to_all x1 -> x0, blocking collectives: 47.9 us -> none  [body(): lax.all_to_all(jnp.repeat(packed, copies, axis=0), 'ep', split_axis=0, co...]
    dot_general x4 -> x1, matrix products: 45.8 us -> 5.9 us  [body(): jnp.einsum('bcr,brf->bcf', onehot, gathered, preferred_element_type=jnp.f...]
    all_to_all x1, waiting for transfers between devices: 24.2 us -> 13.3 us  [body(): lax.all_to_all(partial_value.reshape(n_ep, CAP, -1), 'ep', split_axis=0,...]
  transfers between devices with their start and end apart: 3 -> 1, of which waited for: 3 -> 1; matrix products, arithmetic and copies ran while one was open for 0% -> 0% of each run, Pallas kernels for 0% -> 0%
where the time goes in v1:
time: 166 us
  Pallas kernels  138 us (83%)
  waiting for transfers between devices  13.3 us (8%)
  matrix products  7.48 us (5%)
  starting transfers between devices  3.52 us (2%)
  other arithmetic  1.98 us (1%)
    pallas_call x1, Pallas kernels, ffn(): pl.pallas_call(functools.partial(ffn_kernel, n_tp, cols), out_shape=jax.S...  96.8 us
    pallas_call x1, Pallas kernels, gather_tokens(): pl.pallas_call(functools.partial(gather_kernel, n_ep, n_tp, halves), out_...  41.5 us
    all_to_all x1, waiting for transfers between devices, body(): lax.all_to_all(partial_value.reshape(n_ep, CAP, -1), 'ep', split_axis=0,...  13.3 us
    dot_general x1, matrix products, body(): jnp.einsum('bcr,brf->bcf', onehot, gathered, preferred_element_type=jnp.f...  5.9 us
    all_to_all x1, starting transfers between devices, body(): lax.all_to_all(partial_value.reshape(n_ep, CAP, -1), 'ep', split_axis=0,...  3.52 us
  transfers between devices with their start and end apart: 1, of which 1 were waited for; matrix products, arithmetic and copies ran while one was open for 0% of the time, Pallas kernels for 0%

profile of v1, /device:TPU:0, one launch (start us, length us, event | category | flops | bytes accessed | tf_op | source)
XLA Modules:
  0.0 166.1 jit_solution(13988221574188371939)
XLA Ops:
  0.7 0.7 select_bitcast_fusion
  1.4 0.6 scatter.4.meta
  2.0 41.5 %gather_tokens.1 = (bf16[4,128,6144]{2,1,0:T(8,128)(2,1)}, s32[4,8,128]{2,1,0:T(8,128)}) custom-call(bf16[128,1536]{1,0:T(8,128)(2,1)} %tok.1, s32[8,128]{1,0:T(8,128)} %scatter.4.meta), custom_call_target="tpu_custom_call" | custom-call | tf_op jit(solution)/shard_map/gather_tokens/pallas_call | solution.py:152
  43.4 0.7 compare_reduce_fusion
  44.2 0.3 reduce_window_sum.23
  44.5 5.9 %convolution_convert_fusion = bf16[4,80,6144]{2,1,0:T(8,128)(2,1)} fusion(bf16[4,128,6144]{2,1,0:T(8,128)(2,1)} %get-tuple-element.20, s32[4,128]{1,0:T(4,128)S(1)} %broadcast_add_fusion, pred[4,128]{1,0:T(4,128)(4,1)S(1)} %compare_reduce_fusion), kind=kOutput, calls=%fused_computation | convolution fusion | flops 505364480 | bytes 10226176 | tf_op jit(solution)/shard_map/bcr,brf->bcf/dot_general | solution.py:327
  50.4 0.0 copy-start
  50.4 0.0 copy-start.1
  50.4 96.8 %ffn.1 = bf16[320,1536]{1,0:T(8,128)(2,1)} custom-call(bf16[320,6144]{1,0:T(8,128)(2,1)} %bitcast.17, bf16[6144,2048]{1,0:T(8,128)(2,1)} %gate.1, bf16[6144,2048]{1,0:T(8,128)(2,1)} %up.1, bf16[8192,1536]{1,0:T(8,128)(2,1)} %down.1), custom_call_target="tpu_custom_call" | custom-call | flops 24159191040 | bytes 75497472 | tf_op jit(solution)/shard_map/ffn/pallas_call | solution.py:294
  147.2 3.5 %all-to-all-start = ((bf16[4,80,1536]{2,1,0:T(8,128)(2,1)}), bf16[4,80,1536]{2,1,0:T(8,128)(2,1)S(1)}, u32[]{:S(2)}, u32[]{:S(2)}) async-start(bf16[4,80,1536]{2,1,0:T(8,128)(2,1)} %bitcast.18), calls=%async_computation | async-start | bytes 1966080 | tf_op jit(solution)/shard_map/all_to_all | solution.py:331
  150.8 0.0 copy-done
  150.8 0.1 copy.12
  150.9 0.2 reduce_window_sum.22
  151.1 0.1 copy.13
  151.2 0.0 copy-done.1
  151.2 13.3 %all-to-all-done = bf16[4,80,1536]{2,1,0:T(8,128)(2,1)S(1)} async-done(((bf16[4,80,1536]{2,1,0:T(8,128)(2,1)}), bf16[4,80,1536]{2,1,0:T(8,128)(2,1)S(1)}, u32[]{:S(2)}, u32[]{:S(2)}) %all-to-all-start) | async-done | bytes 983072 | tf_op jit(solution)/shard_map/all_to_all | solution.py:331
  164.5 1.6 fusion
  (7 shorter events, 0.1 us)
Async XLA Ops:
  50.4 100.4 %copy-start = (s32[128,2]{0,1:T(2,128)S(1)}, s32[128,2]{0,1:T(2,128)}, u32[]{:S(2)}) copy-start(s32[128,2]{0,1:T(2,128)} %param.10) | copy-start | bytes 3076
  50.4 100.8 %copy-start.1 = (f32[128,2]{0,1:T(2,128)S(1)}, f32[128,2]{0,1:T(2,128)}, u32[]{:S(2)}) copy-start(f32[128,2]{0,1:T(2,128)} %param.11) | copy-start | bytes 3076
  147.2 17.3 %all-to-all-start = ((bf16[4,80,1536]{2,1,0:T(8,128)(2,1)}), bf16[4,80,1536]{2,1,0:T(8,128)(2,1)S(1)}, u32[]{:S(2)}, u32[]{:S(2)}) async-start(bf16[4,80,1536]{2,1,0:T(8,128)(2,1)} %bitcast.18), calls=%async_computation | async-start | bytes 1966080 | tf_op jit(solution)/shard_map/all_to_all | solution.py:331

commit v2 on v1

--- a/solution.py
+++ b/solution.py
@@ -162,10 +162,22 @@
     )(tokens, meta)
 
 
-def ffn_kernel(n_tp, cols, x, gate, up, down, out, wg, wu, wd, hid, acc, w_sem, d_sem, r_send, l_send, recv):
+def ffn_kernel(n_ep, n_tp, cols, tokens, onehot, gate, up, down, ret, x, held, wg, wu, wd, hid, acc, done,
+               t_sem, w_sem, d_sem, r_send, l_send, recv, b_send, b_recv, o_send, o_recv):
     z = lax.axis_index("tp")
+    b = lax.axis_index("ep")
+    chips = n_ep // 2
+    others = [lax.rem(b + j, n_ep) for j in range(1, n_ep)]
     steps = hid.shape[1]
     depth = steps * cols
+    width = x.shape[1]
+    strip = width // 4
+
+    def order(i):
+        return 2 * lax.rem(b // 2 + 1 + i // 2, chips) + lax.rem(b + 1 + i, 2)
+
+    def rows_of(block):
+        return pl.ds(pl.multiple_of(block * CAP, 16), CAP)
 
     def fetch(c, slot):
         at = pl.ds(pl.multiple_of(c * cols, 128), cols)
@@ -176,6 +188,9 @@
         at = pl.ds(pl.multiple_of(s * depth, 128), depth)
         return pltpu.make_async_copy(down.at[at, :], wd.at[at, :], d_sem.at[s])
 
+    def fetch_tokens(block, slot):
+        return pltpu.make_async_copy(tokens.at[block], held.at[slot], t_sem.at[slot])
+
     def send(s, c, sem, to):
         return pltpu.make_async_remote_copy(
             src_ref=hid.at[s, c], dst_ref=hid.at[s, c], send_sem=sem.at[s, c], recv_sem=recv.at[s, c],
@@ -187,21 +202,49 @@
     def left(s, c):
         return send(s, c, l_send, z - 1)
 
+    def block_send(s, block, way, to):
+        at = hid.at[s, :, rows_of(block), :]
+        return pltpu.make_async_remote_copy(
+            src_ref=at, dst_ref=at, send_sem=b_send.at[way, block], recv_sem=b_recv.at[block],
+            device_id={"tp": to}, device_id_type=MESH)
+
+    def back(block, source):
+        return pltpu.make_async_remote_copy(
+            src_ref=done.at[block], dst_ref=ret.at[source], send_sem=o_send.at[block], recv_sem=o_recv.at[source],
+            device_id={"ep": block}, device_id_type=MESH)
+
+    fetch_tokens(0, 0).start()
     for copy in fetch(0, 0):
         copy.start()
+
+    barrier = pltpu.get_barrier_semaphore()
+    for other in others:
+        pl.semaphore_signal(barrier, inc=1, device_id={"ep": other}, device_id_type=MESH)
+
+    @pl.when(z > 0)
+    def _():
+        pl.semaphore_signal(barrier, inc=1, device_id={"tp": z - 1}, device_id_type=MESH)
+
+    @pl.when(z < n_tp - 1)
+    def _():
+        pl.semaphore_signal(barrier, inc=1, device_id={"tp": z + 1}, device_id_type=MESH)
+
+    @pl.loop(0, n_ep)
+    def _(block):
+        slot = lax.rem(block, 2)
+
+        @pl.when(block + 1 < n_ep)
+        def _():
+            fetch_tokens(block + 1, 1 - slot).start()
+
+        fetch_tokens(block, slot).wait()
+        for j in range(4):
+            at = pl.ds(j * strip, strip)
+            x[rows_of(block), at] = jnp.dot(
+                onehot[block], held[slot, :, at], preferred_element_type=jnp.float32).astype(x.dtype)
+
     acc[...] = jnp.zeros_like(acc)
-
-    barrier = pltpu.get_barrier_semaphore()
-
-    @pl.when(z > 0)
-    def _():
-        pl.semaphore_signal(barrier, inc=1, device_id={"tp": z - 1}, device_id_type=MESH)
-
-    @pl.when(z < n_tp - 1)
-    def _():
-        pl.semaphore_signal(barrier, inc=1, device_id={"tp": z + 1}, device_id_type=MESH)
-
-    pl.semaphore_wait(barrier, jnp.minimum(z, 1) + jnp.minimum(n_tp - 1 - z, 1))
+    pl.semaphore_wait(barrier, n_ep - 1 + jnp.minimum(z, 1) + jnp.minimum(n_tp - 1 - z, 1))
 
     @pl.loop(0, steps)
     def _(c):
@@ -231,14 +274,22 @@
             for s in range(n_tp):
                 fetch_down(s).start()
 
-    for s in range(n_tp):
-        fetch_down(s).wait()
+    def weights_of(s, c):
+        return wd[pl.ds(pl.multiple_of(s * depth + c * cols, 128), cols), :]
 
     def add(s, c):
-        at = pl.ds(pl.multiple_of(s * depth + c * cols, 128), cols)
-        acc[...] += jnp.dot(hid[s, c], wd[at, :], preferred_element_type=jnp.float32)
-
-    for k in range(1, n_tp):
+        acc[...] += jnp.dot(hid[s, c], weights_of(s, c), preferred_element_type=jnp.float32)
+
+    def finish(i):
+        block = order(i)
+        value = acc[rows_of(block), :].astype(ret.dtype)
+        if i == n_ep - 1:
+            ret[b] = value
+        else:
+            done[block] = value
+            back(block, b).start()
+
+    for k in range(1, n_tp - 1):
         @pl.loop(0, steps)
         def _(c):
             @pl.when(z - k >= 0)
@@ -247,7 +298,13 @@
 
                 @pl.when(z < n_tp - 1)
                 def _():
-                    right(z - k, c).start()
+                    if k < n_tp - 2:
+                        right(z - k, c).start()
+                    else:
+                        @pl.when(c == steps - 1)
+                        def _():
+                            for i in range(n_ep):
+                                block_send(z - k, order(i), 0, z + 1).start()
 
             @pl.when(z + k < n_tp)
             def _():
@@ -255,9 +312,20 @@
 
                 @pl.when(z > 0)
                 def _():
-                    left(z + k, c).start()
+                    if k < n_tp - 2:
+                        left(z + k, c).start()
+                    else:
+                        @pl.when(c == steps - 1)
+                        def _():
+                            for i in range(n_ep):
+                                block_send(z + k, order(i), 1, z - 1).start()
 
             if k == 1:
+                @pl.when(c == 0)
+                def _():
+                    for s in range(n_tp):
+                        fetch_down(s).wait()
+
                 add(z, c)
 
             @pl.when(z - k >= 0)
@@ -268,23 +336,56 @@
             def _():
                 add(z + k, c)
 
-    out[...] = acc[...].astype(out.dtype)
+    at_end = (z == 0) | (z == n_tp - 1)
+
+    @pl.when(at_end)
+    def _():
+        far = n_tp - 1 - z
+        for i in range(n_ep):
+            block = order(i)
+            block_send(far, block, 0, jnp.where(z == 0, 1, z - 1)).wait_recv()
+
+            @pl.loop(0, steps)
+            def _(c):
+                acc[rows_of(block), :] += jnp.dot(
+                    hid[far, c, rows_of(block), :], weights_of(far, c), preferred_element_type=jnp.float32)
+
+            finish(i)
+
+    @pl.when(jnp.logical_not(at_end))
+    def _():
+        for i in range(n_ep):
+            finish(i)
 
     @pl.loop(0, steps)
     def _(c):
         for s in range(n_tp):
-            @pl.when((z < n_tp - 1) & (s <= z))
+            @pl.when((z < n_tp - 1) & (s <= z) & ((s > 0) | (z < n_tp - 2)))
             def _():
                 right(s, c).wait_send()
 
-            @pl.when((z > 0) & (s >= z))
+            @pl.when((z > 0) & (s >= z) & ((s < n_tp - 1) | (z > 1)))
             def _():
                 left(s, c).wait_send()
 
-
-def ffn(x, gate, up, down, n_tp):
-    rows, width = x.shape
-    hidden = gate.shape[1]
+    for i in range(n_ep):
+        @pl.when(z == n_tp - 2)
+        def _():
+            block_send(0, order(i), 0, z + 1).wait_send()
+
+        @pl.when(z == 1)
+        def _():
+            block_send(n_tp - 1, order(i), 1, z - 1).wait_send()
+
+    for other in others:
+        back(other, other).wait_recv()
+        back(other, b).wait_send()
+
+
+def ffn(tokens, onehot, gate, up, down, n_ep, n_tp):
+    width, hidden = gate.shape
+    rows = n_ep * CAP
+    out_width = down.shape[1]
     cols = min(256, hidden)
     steps = hidden // cols
     dma = pltpu.SemaphoreType.DMA
@@ -292,23 +393,27 @@
     vmem = pl.BlockSpec(memory_space=pltpu.VMEM)
     bf16 = jnp.bfloat16
     return pl.pallas_call(
-        functools.partial(ffn_kernel, n_tp, cols),
-        out_shape=jax.ShapeDtypeStruct((rows, down.shape[1]), bf16),
-        in_specs=[vmem, hbm, hbm, hbm],
+        functools.partial(ffn_kernel, n_ep, n_tp, cols),
+        out_shape=jax.ShapeDtypeStruct((n_ep, CAP, out_width), bf16),
+        in_specs=[hbm, vmem, hbm, hbm, hbm],
         out_specs=vmem,
         scratch_shapes=[
+            pltpu.VMEM((rows, width), bf16),
+            pltpu.VMEM((2,) + tokens.shape[1:], bf16),
             pltpu.VMEM((2, width, cols), bf16), pltpu.VMEM((2, width, cols), bf16),
             pltpu.VMEM(down.shape, bf16),
             pltpu.VMEM((n_tp, steps, rows, cols), bf16),
-            pltpu.VMEM((rows, down.shape[1]), jnp.float32),
-            dma((2, 2)), dma((n_tp,)), dma((n_tp, steps)), dma((n_tp, steps)), dma((n_tp, steps))],
+            pltpu.VMEM((rows, out_width), jnp.float32),
+            pltpu.VMEM((n_ep, CAP, out_width), bf16),
+            dma((2,)), dma((2, 2)), dma((n_tp,)), dma((n_tp, steps)), dma((n_tp, steps)), dma((n_tp, steps)),
+            dma((2, n_ep)), dma((n_ep,)), dma((n_ep,)), dma((n_ep,))],
         compiler_params=pltpu.CompilerParams(
             collective_id=1, has_side_effects=True, vmem_limit_bytes=60 * 1024 * 1024),
         cost_estimate=pl.CostEstimate(
             flops=2 * rows * (2 * width * hidden + down.size),
             bytes_accessed=2 * (gate.size + up.size + down.size), transcendentals=rows * hidden),
         name="ffn",
-    )(x, gate, up, down)
+    )(tokens, onehot, gate, up, down)
 
 
 def body(tokens, picks, gates, counts, gate_weight, up_weight, down_weight):
@@ -324,12 +429,7 @@
     routed = jnp.any(meta_all[:, :2] == expert, axis=1)
     rank = jnp.cumsum(routed.astype(jnp.int32), axis=1) - 1
     onehot = (routed[:, None] & (rank[:, None] == slots[None, :, None])).astype(jnp.bfloat16)
-    packed = jnp.einsum("bcr,brf->bcf", onehot, gathered, preferred_element_type=jnp.float32)
-    packed = packed.astype(jnp.bfloat16).reshape(n_ep * CAP, -1)
-
-    partial_value = ffn(packed, gate_weight, up_weight, down_weight, n_tp)
-    returned = lax.all_to_all(
-        partial_value.reshape(n_ep, CAP, -1), "ep", split_axis=0, concat_axis=0, tiled=True)
+    returned = ffn(gathered, onehot, gate_weight, up_weight, down_weight, n_ep, n_tp)
 
     matches = picks[:, :, None] == jnp.arange(E, dtype=jnp.int32)
     own_routed = jnp.any(matches, axis=1) & live[:, None]

time: 166 us -> 152 us (0.916)
  waiting for transfers between devices: 13.3 us -> 0 us
  Pallas kernels: 138 us -> 145 us
  matrix products: 7.48 us -> 2.78 us
  starting transfers between devices: 3.52 us -> 0 us
    all_to_all x1 -> x0, waiting for transfers between devices: 13.3 us -> none  [body(): lax.all_to_all(partial_value.reshape(n_ep, CAP, -1), 'ep', split_axis=0,...]
    pallas_call x1, Pallas kernels: 96.8 us -> 103 us  [ffn(): pl.pallas_call(functools.partial(ffn_kernel, n_ep, n_tp, cols), out_shape...]
    dot_general x1 -> x0, matrix products: 5.9 us -> none  [body(): jnp.einsum('bcr,brf->bcf', onehot, gathered, preferred_element_type=jnp.f...]
    all_to_all x1 -> x0, starting transfers between devices: 3.52 us -> none  [body(): lax.all_to_all(partial_value.reshape(n_ep, CAP, -1), 'ep', split_axis=0,...]
  transfers between devices with their start and end apart: 1 -> 0, of which waited for: 1 -> 0; matrix products, arithmetic and copies ran while one was open for 0% -> 0% of each run, Pallas kernels for 0% -> 0%
where the time goes in v2:
time: 152 us; the launch traced here: 151 us
  Pallas kernels  145 us (95%)
  matrix products  2.78 us (2%)
  other arithmetic  2.65 us (2%)
    pallas_call x1, Pallas kernels, ffn(): pl.pallas_call(functools.partial(ffn_kernel, n_ep, n_tp, cols), out_shape...  103 us
    pallas_call x1, Pallas kernels, gather_tokens(): pl.pallas_call(functools.partial(gather_kernel, n_ep, n_tp, halves), out_...  41.5 us

profile of v2, /device:TPU:0, one launch (start us, length us, event | category | flops | bytes accessed | tf_op | source)
XLA Modules:
  0.0 151.5 jit_solution(2022223776720020791)
XLA Ops:
  0.7 0.7 select_bitcast_fusion
  1.4 0.6 scatter.4.meta
  1.9 41.5 %gather_tokens.1 = (bf16[4,128,6144]{2,1,0:T(8,128)(2,1)}, s32[4,8,128]{2,1,0:T(8,128)}) custom-call(bf16[128,1536]{1,0:T(8,128)(2,1)} %tok.1, s32[8,128]{1,0:T(8,128)} %scatter.4.meta), custom_call_target="tpu_custom_call" | custom-call | tf_op jit(solution)/shard_map/gather_tokens/pallas_call | solution.py:152
  43.4 0.7 compare_reduce_fusion
  44.2 0.3 reduce_window_sum.23
  44.5 0.7 fusion.5.onehot
  45.1 0.0 copy-start
  45.2 0.0 copy-start.1
  45.2 103.1 %ffn.1 = bf16[4,80,1536]{2,1,0:T(8,128)(2,1)} custom-call(bf16[4,128,6144]{2,1,0:T(8,128)(2,1)} %get-tuple-element.19.tokens, bf16[4,80,128]{2,1,0:T(8,128)(2,1)} %fusion.5.onehot, bf16[6144,2048]{1,0:T(8,128)(2,1)} %gate.1, bf16[6144,2048]{1,0:T(8,128)(2,1)} %up.1, bf16[8192,1536]{1,0:T(8,128)(2,1)} %down.1), custom_call_target="tpu_custom_call" | custom-call | flops 24159191040 | bytes 75497472 | tf_op jit(solution)/shard_map/ffn/pallas_call | solution.py:395
  148.3 0.0 copy-done
  148.3 0.1 copy.12
  148.4 0.2 reduce_window_sum.22
  148.6 0.1 copy.13
  148.7 0.0 copy-done.1
  148.7 2.8 %fusion = bf16[128,1536]{1,0:T(8,128)(2,1)} fusion(bf16[4,80,1536]{2,1,0:T(8,128)(2,1)} %ffn.1, f32[4,128]{1,0:T(4,128)S(1)} %bitcast.14, s32[4,128]{1,0:T(4,128)S(1)} %copy.13, pred[4,128]{1,0:T(4,128)(4,1)S(1)} %get-tuple-element.21), kind=kOutput, calls=%fused_computation.1 | convolution fusion | flops 755294208 | bytes 1380864 | tf_op jit(solution)/shard_map/ecr,ecf->rf/dot_general | solution.py:441
  (7 shorter events, 0.1 us)
Async XLA Ops:
  45.1 103.1 %copy-start = (s32[128,2]{0,1:T(2,128)S(1)}, s32[128,2]{0,1:T(2,128)}, u32[]{:S(2)}) copy-start(s32[128,2]{0,1:T(2,128)} %param.10) | copy-start | bytes 3076
  45.2 103.5 %copy-start.1 = (f32[128,2]{0,1:T(2,128)S(1)}, f32[128,2]{0,1:T(2,128)}, u32[]{:S(2)}) copy-start(f32[128,2]{0,1:T(2,128)} %param.11) | copy-start | bytes 3076

commit v3 on v2

--- a/solution.py
+++ b/solution.py
@@ -12,7 +12,7 @@
 MESH = pl.DeviceIdType.MESH
 
 
-def gather_kernel(n_ep, n_tp, halves, tok, meta, out, meta_out, local_sem, z_send, x_send, c_send, recv, m_send, m_recv):
+def gather_kernel(n_ep, n_tp, halves, tok, meta, out, meta_out, local_sem, z_send, turn_send, x_send, c_send, recv, m_send, m_recv):
     z = lax.axis_index("tp")
     b = lax.axis_index("ep")
     chips = n_ep // 2
@@ -65,9 +65,14 @@
 
     pl.semaphore_wait(barrier, n_ep - 1 + jnp.minimum(z, 1) + jnp.minimum(n_tp - 1 - z, 1))
 
-    def fan_out(p, h, own):
-        for j in range(chips - 1):
-            across(j, p, h, own).start()
+    def turn(block, way):
+        return copy(block, z, 1, False, turn_send.at[way, block], {"tp": z + 1 - 2 * way})
+
+    def fan_out(p, h, k):
+        own = k == 0
+        if not (k == 1 and h == 1):
+            for j in range(chips - 1):
+                across(j, p, h, own).start()
         to_core(b, p, h, own).start()
 
     for h in range(halves):
@@ -79,7 +84,7 @@
         def _():
             left(z, h, True).start()
 
-        fan_out(z, h, True)
+        fan_out(z, h, 0)
     for j in range(n_ep - 1):
         meta_copy(j).start()
     local.start()
@@ -91,6 +96,15 @@
             def _():
                 for block in peers:
                     to_core(block, p, h).wait_recv()
+                    if k == 0 and h == 1:
+                        @pl.when(z < n_tp - 1)
+                        def _():
+                            turn(block, 0).start()
+
+                        @pl.when(z > 0)
+                        def _():
+                            turn(block, 1).start()
+
                     to_core(block, p, h).start()
 
     for k in range(1, n_tp):
@@ -103,7 +117,7 @@
                 def _():
                     right(z - k, h).start()
 
-                fan_out(z - k, h, False)
+                fan_out(z - k, h, k)
 
             @pl.when(z + k < n_tp)
             def _():
@@ -113,7 +127,7 @@
                 def _():
                     left(z + k, h).start()
 
-                fan_out(z + k, h, False)
+                fan_out(z + k, h, k)
 
             pass_to_core(k - 1, h)
     for h in range(halves):
@@ -125,8 +139,14 @@
                 to_core(block, p, h).wait_recv()
             for block in [b] + peers:
                 to_core(block, p, h).wait_send()
-            for j in range(chips - 1):
-                across(j, p, h).wait_send()
+            if h == 1:
+                @pl.when((p != z - 1) & (p != z + 1))
+                def _():
+                    for j in range(chips - 1):
+                        across(j, p, h).wait_send()
+            else:
+                for j in range(chips - 1):
+                    across(j, p, h).wait_send()
 
             @pl.when((z < n_tp - 1) & (p <= z))
             def _():
@@ -135,6 +155,16 @@
             @pl.when((z > 0) & (p >= z))
             def _():
                 left(p, h).wait_send()
+    if halves > 1:
+        for block in peers:
+            @pl.when(z < n_tp - 1)
+            def _():
+                turn(block, 0).wait_send()
+
+            @pl.when(z > 0)
+            def _():
+                turn(block, 1).wait_send()
+
     for j in range(n_ep - 1):
         meta_copy(j).wait_send()
         pltpu.make_async_remote_copy(
@@ -155,7 +185,7 @@
                    jax.ShapeDtypeStruct((n_ep,) + meta.shape, meta.dtype)),
         in_specs=[hbm, hbm],
         out_specs=(hbm, hbm),
-        scratch_shapes=[dma((2,)), dma((2, n_tp, halves)), dma((max(1, n_ep // 2 - 1), n_tp, halves)),
+        scratch_shapes=[dma((2,)), dma((2, n_tp, halves)), dma((2, n_ep)), dma((max(1, n_ep // 2 - 1), n_tp, halves)),
                         dma((n_ep, n_tp, halves)), dma((n_ep, n_tp, halves)), dma((n_ep,)), dma((n_ep,))],
         compiler_params=pltpu.CompilerParams(collective_id=0, has_side_effects=True),
         name="gather_tokens",
@@ -280,6 +310,18 @@
     def add(s, c):
         acc[...] += jnp.dot(hid[s, c], weights_of(s, c), preferred_element_type=jnp.float32)
 
+    def add_at(k, c):
+        if k == 0:
+            add(z, c)
+        else:
+            @pl.when(z - k >= 0)
+            def _():
+                add(z - k, c)
+
+            @pl.when(z + k < n_tp)
+            def _():
+                add(z + k, c)
+
     def finish(i):
         block = order(i)
         value = acc[rows_of(block), :].astype(ret.dtype)
@@ -326,15 +368,11 @@
                     for s in range(n_tp):
                         fetch_down(s).wait()
 
-                add(z, c)
-
-            @pl.when(z - k >= 0)
-            def _():
-                add(z - k, c)
-
-            @pl.when(z + k < n_tp)
-            def _():
-                add(z + k, c)
+            add_at(k - 1, c)
+
+    @pl.loop(0, steps)
+    def _(c):
+        add_at(n_tp - 2, c)
 
     at_end = (z == 0) | (z == n_tp - 1)
 

time: 152 us -> 148 us (0.974)
  Pallas kernels: 145 us -> 141 us
    pallas_call x1, Pallas kernels: 103 us -> 96.8 us  [ffn(): pl.pallas_call(functools.partial(ffn_kernel, n_ep, n_tp, cols), out_shape...]
    pallas_call x1, Pallas kernels: 41.5 us -> 43.8 us  [gather_tokens(): pl.pallas_call(functools.partial(gather_kernel, n_ep, n_tp, halves), out_...]
where the time goes in v3:
time: 148 us
  Pallas kernels  141 us (95%)
  matrix products  2.78 us (2%)
  other arithmetic  2.65 us (2%)
    pallas_call x1, Pallas kernels, ffn(): pl.pallas_call(functools.partial(ffn_kernel, n_ep, n_tp, cols), out_shape...  96.8 us
    pallas_call x1, Pallas kernels, gather_tokens(): pl.pallas_call(functools.partial(gather_kernel, n_ep, n_tp, halves), out_...  43.8 us

profile of v3, /device:TPU:0, one launch (start us, length us, event | category | flops | bytes accessed | tf_op | source)
XLA Modules:
  0.0 147.5 jit_solution(12438387508649395658)
XLA Ops:
  0.7 0.7 select_bitcast_fusion
  1.4 0.6 scatter.4.meta
  1.9 43.8 %gather_tokens.1 = (bf16[4,128,6144]{2,1,0:T(8,128)(2,1)}, s32[4,8,128]{2,1,0:T(8,128)}) custom-call(bf16[128,1536]{1,0:T(8,128)(2,1)} %tok.1, s32[8,128]{1,0:T(8,128)} %scatter.4.meta), custom_call_target="tpu_custom_call" | custom-call | tf_op jit(solution)/shard_map/gather_tokens/pallas_call | solution.py:182
  45.8 0.7 compare_reduce_fusion
  46.5 0.3 reduce_window_sum.23
  46.8 0.7 fusion.5.onehot
  47.5 0.0 copy-start
  47.5 0.0 copy-start.1
  47.5 96.8 %ffn.1 = bf16[4,80,1536]{2,1,0:T(8,128)(2,1)} custom-call(bf16[4,128,6144]{2,1,0:T(8,128)(2,1)} %get-tuple-element.19.tokens, bf16[4,80,128]{2,1,0:T(8,128)(2,1)} %fusion.5.onehot, bf16[6144,2048]{1,0:T(8,128)(2,1)} %gate.1, bf16[6144,2048]{1,0:T(8,128)(2,1)} %up.1, bf16[8192,1536]{1,0:T(8,128)(2,1)} %down.1), custom_call_target="tpu_custom_call" | custom-call | flops 24159191040 | bytes 75497472 | tf_op jit(solution)/shard_map/ffn/pallas_call | solution.py:433
  144.3 0.0 copy-done
  144.3 0.1 copy.12
  144.5 0.2 reduce_window_sum.22
  144.6 0.1 copy.13
  144.7 0.0 copy-done.1
  144.7 2.8 %fusion = bf16[128,1536]{1,0:T(8,128)(2,1)} fusion(bf16[4,80,1536]{2,1,0:T(8,128)(2,1)} %ffn.1, f32[4,128]{1,0:T(4,128)S(1)} %bitcast.14, s32[4,128]{1,0:T(4,128)S(1)} %copy.13, pred[4,128]{1,0:T(4,128)(4,1)S(1)} %get-tuple-element.21), kind=kOutput, calls=%fused_computation.1 | convolution fusion | flops 755294208 | bytes 1380864 | tf_op jit(solution)/shard_map/ecr,ecf->rf/dot_general | solution.py:479
  (7 shorter events, 0.1 us)
Async XLA Ops:
  47.5 96.8 %copy-start = (s32[128,2]{0,1:T(2,128)S(1)}, s32[128,2]{0,1:T(2,128)}, u32[]{:S(2)}) copy-start(s32[128,2]{0,1:T(2,128)} %param.10) | copy-start | bytes 3076
  47.5 97.2 %copy-start.1 = (f32[128,2]{0,1:T(2,128)S(1)}, f32[128,2]{0,1:T(2,128)}, u32[]{:S(2)}) copy-start(f32[128,2]{0,1:T(2,128)} %param.11) | copy-start | bytes 3076

commit v4 on v3

--- a/solution.py
+++ b/solution.py
@@ -129,6 +129,7 @@
 
                 fan_out(z + k, h, k)
 
+        for h in range(halves):
             pass_to_core(k - 1, h)
     for h in range(halves):
         pass_to_core(n_tp - 1, h)

time: 148 us -> 148 us (level)
  no operation moved by 1% of the time
where the time goes in v4:
time: 148 us
  Pallas kernels  141 us (95%)
  matrix products  2.78 us (2%)
  other arithmetic  2.65 us (2%)
    pallas_call x1, Pallas kernels, ffn(): pl.pallas_call(functools.partial(ffn_kernel, n_ep, n_tp, cols), out_shape...  96.8 us
    pallas_call x1, Pallas kernels, gather_tokens(): pl.pallas_call(functools.partial(gather_kernel, n_ep, n_tp, halves), out_...  43.8 us

profile of v4, /device:TPU:0, one launch (start us, length us, event | category | flops | bytes accessed | tf_op | source)
XLA Modules:
  0.0 147.5 jit_solution(5251927819165155519)
XLA Ops:
  0.7 0.7 select_bitcast_fusion
  1.4 0.6 scatter.4.meta
  1.9 43.8 %gather_tokens.1 = (bf16[4,128,6144]{2,1,0:T(8,128)(2,1)}, s32[4,8,128]{2,1,0:T(8,128)}) custom-call(bf16[128,1536]{1,0:T(8,128)(2,1)} %tok.1, s32[8,128]{1,0:T(8,128)} %scatter.4.meta), custom_call_target="tpu_custom_call" | custom-call | tf_op jit(solution)/shard_map/gather_tokens/pallas_call | solution.py:183
  45.8 0.7 compare_reduce_fusion
  46.5 0.3 reduce_window_sum.23
  46.8 0.7 fusion.5.onehot
  47.5 0.0 copy-start
  47.5 0.0 copy-start.1
  47.5 96.8 %ffn.1 = bf16[4,80,1536]{2,1,0:T(8,128)(2,1)} custom-call(bf16[4,128,6144]{2,1,0:T(8,128)(2,1)} %get-tuple-element.19.tokens, bf16[4,80,128]{2,1,0:T(8,128)(2,1)} %fusion.5.onehot, bf16[6144,2048]{1,0:T(8,128)(2,1)} %gate.1, bf16[6144,2048]{1,0:T(8,128)(2,1)} %up.1, bf16[8192,1536]{1,0:T(8,128)(2,1)} %down.1), custom_call_target="tpu_custom_call" | custom-call | flops 24159191040 | bytes 75497472 | tf_op jit(solution)/shard_map/ffn/pallas_call | solution.py:434
  144.3 0.0 copy-done
  144.3 0.1 copy.12
  144.5 0.2 reduce_window_sum.22
  144.6 0.1 copy.13
  144.7 0.0 copy-done.1
  144.7 2.8 %fusion = bf16[128,1536]{1,0:T(8,128)(2,1)} fusion(bf16[4,80,1536]{2,1,0:T(8,128)(2,1)} %ffn.1, f32[4,128]{1,0:T(4,128)S(1)} %bitcast.14, s32[4,128]{1,0:T(4,128)S(1)} %copy.13, pred[4,128]{1,0:T(4,128)(4,1)S(1)} %get-tuple-element.21), kind=kOutput, calls=%fused_computation.1 | convolution fusion | flops 755294208 | bytes 1380864 | tf_op jit(solution)/shard_map/ecr,ecf->rf/dot_general | solution.py:480
  (7 shorter events, 0.1 us)
Async XLA Ops:
  47.5 96.8 %copy-start = (s32[128,2]{0,1:T(2,128)S(1)}, s32[128,2]{0,1:T(2,128)}, u32[]{:S(2)}) copy-start(s32[128,2]{0,1:T(2,128)} %param.10) | copy-start | bytes 3076
  47.5 97.2 %copy-start.1 = (f32[128,2]{0,1:T(2,128)S(1)}, f32[128,2]{0,1:T(2,128)}, u32[]{:S(2)}) copy-start(f32[128,2]{0,1:T(2,128)} %param.11) | copy-start | bytes 3076
